TPU v7x, 32 devices: a whole 2x2x4 slice. The times are simulated.
32 devices in a mesh: parts: 1, row: 8 (over z, y), col: 1, depth: 4 (over x, core).
Axes of the slice: x: 2, y: 2, z: 4, core: 2. Of those that a mesh axis runs over, the one named last changes fastest.
Arguments:
- activations: bfloat16 [4, 256, 8192], P(('parts', 'depth'), 'row', 'col'), may hold values from -6 to 6
- hidden_grads: bfloat16 [4, 256, 16384], P(('parts', 'depth'), 'col', 'row'), may hold values from -0.1875 to 0.1875
Outputs:
- weight_grad: bfloat16 [8192, 16384], P(('parts', 'col', 'depth'), 'row')
All inputs are finite; a program needn't handle non-finite values.
Results may differ from a plain program's by a relative error of at most 0.013.
Values may be sent and summed in bfloat16 or wider, within the bound.
A program may use at most 128 MiB of HBM per device.

v0:
```python
import jax
import jax.numpy as jnp
from jax import lax
from jax.sharding import PartitionSpec as P


def local(activations, hidden_grads):
    swapped = lax.all_to_all(activations, "depth", split_axis=2, concat_axis=0, tiled=True)
    acts = lax.all_gather(swapped, "row", axis=1, tiled=True)
    grads = lax.all_gather(hidden_grads, "depth", axis=0, tiled=True)
    grads = lax.all_gather(grads, "col", axis=1, tiled=True)
    total = lax.dot_general(
        acts, grads, (((0, 1), (0, 1)), ((), ())), preferred_element_type=jnp.float32
    )
    return total.astype(jnp.bfloat16)


def solution(mesh):
    in_specs = (P(("parts", "depth"), "row", "col"), P(("parts", "depth"), "col", "row"))
    out_specs = P(("parts", "col", "depth"), "row")
    return jax.shard_map(local, mesh=mesh, in_specs=in_specs, out_specs=out_specs, check_vma=False)
```

profile of v0, /device:TPU:0, one launch (start us, length us, event | category | flops | bytes accessed | tf_op | source)
XLA Modules:
  0.0 217.2 jit_solution(3695399159835913625)
XLA Ops:
  6.5 0.0 all-gather.6.cloned.1.call-start
  6.5 8.6 %copy.7 = bf16[1,32,8192]{1,0,2:T(2,128)(2,1)} copy(bf16[1,32,8192]{2,1,0:T(8,128)(2,1)} %param.2) | data formatting | bytes 1048576 | tf_op args[0]
  15.1 0.5 broadcast
  15.6 45.2 %reduce = bf16[8192,32]{1,0:T(8,128)(2,1)S(1)} reduce(bf16[8192,1,32]{2,1,0:T(2,128)(2,1)} %bitcast.11, bf16[]{:T(256)} %broadcast), dimensions={1}, to_apply=%bitcast.8.reduce_sub_computation | reduce | bytes 1048578
  60.8 2.2 reshape.2
  63.0 12.9 %all_to_all.18 = bf16[4,2,32768]{2,1,0:T(2,128)(2,1)S(1)} all-to-all(bf16[4,2,32768]{2,1,0:T(2,128)(2,1)S(1)} %reshape.2), channel_id=1, replica_groups=mesh['parts'=1,'row'=8,'col'=1,'depth'=4] {'depth'}, dimensions={0} | all-to-all | bytes 1048576 | tf_op jit(solution)/shard_map/all_to_all | solution.py:8
  75.9 3.3 %reshape.3 = bf16[8192,1,32]{2,1,0:T(2,128)(2,1)} reshape(bf16[4,2,32768]{2,1,0:T(2,128)(2,1)S(1)} %all_to_all.18) | data formatting | bytes 1048576
  79.1 8.0 %copy.8 = bf16[1,32,8192]{2,1,0:T(8,128)(2,1)S(1)} copy(bf16[1,32,8192]{1,0,2:T(2,128)(2,1)} %bitcast.12) | data formatting | bytes 1048576 | tf_op jit(solution)/shard_map/all_to_all | solution.py:8
  87.1 1.2 all_to_all.14
  88.3 0.0 all-gather.6.cloned.1.call-update
  88.3 0.2 all-gather.4.cloned.1.call-start
  88.5 0.5 all-gather.4.cloned.1.call-update
  89.0 73.1 %all-gather.6.cloned.1.call-done = bf16[4,1,256,2048]{3,0,1,2:T(4,128)(2,1)} async-done(((bf16[4,1,32,2048]{3,0,1,2:T(4,128)(2,1)}), bf16[4,1,256,2048]{3,0,1,2:T(4,128)(2,1)}) %all-gather.6.cloned.1.call-update) | async-done | bytes 4194320 | tf_op jit(solution)/shard_map/all_gather | solution.py:9
  162.2 7.6 %copy.10 = bf16[4,1,256,2048]{2,3,0,1:T(8,128)(2,1)} copy(bf16[4,1,256,2048]{3,0,1,2:T(4,128)(2,1)} %all-gather.6.cloned.1.call-done) | data formatting | bytes 8388608 | tf_op jit(solution)/shard_map/all_gather | solution.py:9
  169.7 26.8 %all-gather.4.cloned.1.call-done = bf16[4,256,2048]{2,1,0:T(8,128)(2,1)} async-done(((bf16[1,256,2048]{2,1,0:T(8,128)(2,1)}), bf16[4,256,2048]{2,1,0:T(8,128)(2,1)}) %all-gather.4.cloned.1.call-update) | async-done | bytes 4194320 | tf_op jit(solution)/shard_map/all_gather | solution.py:10
  196.5 13.9 %bitcast_convert_fusion = bf16[2048,2048]{1,0:T(8,128)(2,1)} fusion(bf16[4,256,2048]{2,1,0:T(8,128)(2,1)} %all-gather.4.cloned.1.call-done, bf16[4,1,256,2048]{2,3,0,1:T(8,128)(2,1)} %copy.10), kind=kOutput, calls=%fused_computation | convolution fusion | flops 8594128896 | bytes 16777216 | tf_op jit(solution)/shard_map/dot_general | solution.py:12
Async XLA Ops:
  6.5 155.6 %all-gather.6.cloned.1.call-start = ((), (), s32[]{:S(2)}) async-start(), calls=%async_computation.2 | async-start | bytes 4718592 | tf_op jit(solution)/shard_map/all_gather | solution.py:9
  88.3 108.2 %all-gather.4.cloned.1.call-start = ((), (), s32[]{:S(2)}) async-start(), calls=%async_computation.1 | async-start | bytes 5242880 | tf_op jit(solution)/shard_map/all_gather | solution.py:10
Sparse Core Ops, SparseCore 0:
  88.4 73.7 all-gather.5
  163.7 32.7 all-gather.3
where the time goes:
time: 218 us; the launch traced here: 217 us
  waiting for transfers between devices  100 us (46%)
  other arithmetic  45.2 us (21%)
  local copies, waits for them, and re-layouts  31.2 us (14%)
  matrix products  13.9 us (6%)
  between operations  13.4 us (6%)
  blocking collectives  12.9 us (6%)
    all_gather x1, waiting for transfers between devices, local(): acts = lax.all_gather(swapped, 'row', axis=1, tiled=True)  73.1 us
    unnamed x1, other arithmetic  45.2 us
    all_gather x1, waiting for transfers between devices, local(): grads = lax.all_gather(hidden_grads, 'depth', axis=0, tiled=True)  26.8 us
    unnamed x4, local copies, waits for them, and re-layouts  14.5 us
    dot_general x1, matrix products, local(): lax.dot_general(acts, grads, (((0, 1), (0, 1)), ((), ())), preferred_elem...  13.9 us
    all_to_all x1, blocking collectives, local(): lax.all_to_all(activations, 'depth', split_axis=2, concat_axis=0, tiled=T...  12.9 us
    all_to_all x2, local copies, waits for them, and re-layouts, local(): lax.all_to_all(activations, 'depth', split_axis=2, concat_axis=0, tiled=T...  9.14 us
    all_gather x1, local copies, waits for them, and re-layouts, local(): acts = lax.all_gather(swapped, 'row', axis=1, tiled=True)  7.56 us
  transfers between devices with their start and end apart: 2, of which 2 were waited for; matrix products, arithmetic and copies ran while one was open for 3% of the time, Pallas kernels for 0%

commit v1 on v0

v1 whole, which is shorter than its diff:
```python
import functools

import jax
import jax.numpy as jnp
from jax import lax
from jax.experimental import pallas as pl
from jax.experimental.pallas import tpu as pltpu
from jax.sharding import PartitionSpec as P

MESH = pl.DeviceIdType.MESH
MIB = 1024 * 1024
ROWS, COLS, DEPTH = 8, 1, 4
NZ = 4
TILE = 256
SHIFTED = (1, 3)
PARTS = 2


def product_tile(acts, grads, slot, tile):
    cols = pl.ds(pl.multiple_of(tile * TILE, TILE), TILE)
    lhs = acts[slot, :, :, cols]
    lhs = lhs.reshape(lhs.shape[0] * lhs.shape[1], TILE)
    return lax.dot_general(
        lhs, grads[slot], (((0,), (0,)), ((), ())), preferred_element_type=jnp.float32
    )


def gather_kernel(x_hbm, g_hbm, total, acts, grads, local_sem, recv_a, up_sem, down_sem, y_sem, ex_sem, recv_g, send_g):
    row, me = lax.axis_index("row"), lax.axis_index("depth")
    z, y = row // 2, row % 2
    width = acts.shape[3]
    tokens = grads.shape[1]
    one = me + 1 - 2 * (me % 2)
    peers = (me, one, (me + 2) % 4, (one + 2) % 4)
    near = z + 1 - 2 * (z % 2)
    here = 2 * z + y
    across = 2 * z + 1 - y

    def block(k):
        return x_hbm.at[0, :, pl.ds(pl.multiple_of(peers[k] * width, width), width)]

    own_x = pltpu.make_async_copy(block(0), acts.at[0, here], local_sem.at[0])
    own_g = pltpu.make_async_copy(g_hbm.at[0], grads.at[0], local_sem.at[1])
    own_x.start()
    own_g.start()

    barrier = pltpu.get_barrier_semaphore()
    for k in (1, 2, 3):
        pl.semaphore_signal(barrier, inc=1, device_id={"depth": peers[k]}, device_id_type=MESH)
    pl.semaphore_signal(barrier, inc=1, device_id={"row": across}, device_id_type=MESH)

    @pl.when(z > 0)
    def _():
        pl.semaphore_signal(barrier, inc=1, device_id={"row": here - 2}, device_id_type=MESH)

    @pl.when(z < NZ - 1)
    def _():
        pl.semaphore_signal(barrier, inc=1, device_id={"row": here + 2}, device_id_type=MESH)

    pl.semaphore_wait(barrier, 5 + ((z + 1) // 2) % 2)

    def exchange(k):
        return pltpu.make_async_remote_copy(
            block(k), acts.at[k, here], ex_sem.at[k - 1], recv_a.at[k, here],
            device_id={"depth": peers[k]}, device_id_type=MESH,
        )

    def send(j, r, sems, target):
        return pltpu.make_async_remote_copy(
            acts.at[j, r], acts.at[j, r], sems.at[j, r], recv_a.at[j, r],
            device_id={"row": target}, device_id_type=MESH,
        )

    def arrived(j, r):
        send(j, r, y_sem, across).wait_recv()

    part = tokens // PARTS

    def grads_to(k, p):
        rows = pl.ds(p * part, part)
        return pltpu.make_async_remote_copy(
            g_hbm.at[0, rows], grads.at[k, rows], send_g.at[k - 1, p], recv_g.at[k - 1, p],
            device_id={"depth": peers[k]}, device_id_type=MESH,
        )

    def grads_on(p):
        rows = pl.ds(p * part, part)
        return pltpu.make_async_remote_copy(
            grads.at[2, rows], grads.at[3, rows], send_g.at[2, p], recv_g.at[2, p],
            device_id={"depth": peers[1]}, device_id_type=MESH,
        )

    def forward_g(p):
        grads_to(2, p).wait_recv()
        grads_on(p).start()

    def moves(j, origin, go_up, go_down, wait):
        r = 2 * origin + y

        def steps():
            if wait:
                arrived(j, r)
            for going, sems, edge, target in (
                (go_up, up_sem, z < NZ - 1, here + 2),
                (go_down, down_sem, z > 0, here - 2),
            ):
                if going:
                    @pl.when(edge)
                    def _():
                        send(j, r, sems, target).start()
            if j in SHIFTED:
                @pl.when(origin != near)
                def _():
                    send(j, r, y_sem, across).start()
            else:
                send(j, r, y_sem, across).start()

        return steps

    def own(j):
        moves(j, z, True, True, j > 0)()

    def reach(j, dist):
        pl.when(z >= dist)(moves(j, z - dist, True, False, True))
        pl.when(z + dist < NZ)(moves(j, z + dist, False, True, True))

    def turn(j):
        arrived(j, across)
        even = z % 2 == 0

        @pl.when(even)
        def _():
            send(j, across, up_sem, here + 2).start()

        @pl.when(jnp.logical_not(even))
        def _():
            send(j, across, down_sem, here - 2).start()

    def finish(j):
        for origin in range(NZ):
            r = 2 * origin + 1 - y
            if j in SHIFTED:
                @pl.when(z != origin)
                def _():
                    arrived(j, r)
            else:
                arrived(j, r)

    def product(j, first, last):
        @pl.loop(first, last)
        def _(tile):
            rows = pl.ds(pl.multiple_of(tile * TILE, TILE), TILE)
            value = product_tile(acts, grads, j, tile)
            if j == 0:
                total[rows, :] = value
            else:
                total[rows, :] = total[rows, :] + value

    tiles = width // TILE

    own_x.wait()
    own(0)
    exchange(1).start()
    exchange(2).start()
    exchange(3).start()
    for p in range(PARTS):
        grads_to(2, p).start()
    for p in range(PARTS):
        grads_to(1, p).start()
    own(1)
    own_g.wait()
    reach(0, 1)
    own(2)
    reach(1, 1)
    turn(1)
    reach(0, 2)
    own(3)
    reach(2, 1)
    reach(1, 2)
    reach(0, 3)
    forward_g(0)
    turn(3)
    reach(3, 1)
    finish(0)
    product(0, 0, tiles // 4)
    reach(2, 2)
    product(0, tiles // 4, tiles // 2)
    reach(1, 3)
    product(0, tiles // 2, tiles)
    forward_g(1)
    reach(3, 2)
    for p in range(PARTS):
        grads_to(1, p).wait_recv()
    finish(1)
    product(1, 0, tiles // 2)
    reach(2, 3)
    product(1, tiles // 2, tiles)
    reach(3, 3)
    finish(2)
    product(2, 0, tiles)
    finish(3)
    for p in range(PARTS):
        grads_on(p).wait_recv()

    for k in (1, 2, 3):
        exchange(k).wait_send()
    for p in range(PARTS):
        grads_to(1, p).wait_send()
        grads_to(2, p).wait_send()
        grads_on(p).wait_send()
    for j in range(DEPTH):
        for origin in range(NZ):
            mine = 2 * origin + y

            @pl.when(jnp.logical_and(origin <= z, z < NZ - 1))
            def _():
                send(j, mine, up_sem, here + 2).wait_send()

            @pl.when(jnp.logical_and(origin >= z, z > 0))
            def _():
                send(j, mine, down_sem, here - 2).wait_send()

            if j in SHIFTED:
                @pl.when(near != origin)
                def _():
                    send(j, mine, y_sem, across).wait_send()
            else:
                send(j, mine, y_sem, across).wait_send()
        if j in SHIFTED:
            @pl.when(z % 2 == 0)
            def _():
                send(j, across, up_sem, here + 2).wait_send()

            @pl.when(z % 2 == 1)
            def _():
                send(j, across, down_sem, here - 2).wait_send()


def last_kernel(total, acts, grads, out_hbm, held, sems):
    tiles = total.shape[0] // TILE

    def copy(tile, slot):
        rows = pl.ds(pl.multiple_of(tile * TILE, TILE), TILE)
        return pltpu.make_async_copy(held.at[slot], out_hbm.at[rows], sems.at[slot])

    @pl.loop(0, tiles)
    def _(tile):
        slot = tile % 2
        rows = pl.ds(pl.multiple_of(tile * TILE, TILE), TILE)
        value = total[rows, :] + product_tile(acts, grads, DEPTH - 1, tile)

        @pl.when(tile >= 2)
        def _():
            copy(tile - 2, slot).wait()

        held[slot] = value.astype(held.dtype)
        copy(tile, slot).start()

    for tile in (tiles - 2, tiles - 1):
        copy(tile, tile % 2).wait()


def by_kernels(activations, hidden_grads):
    tokens, features = activations.shape[1], activations.shape[2] // DEPTH
    all_tokens, hidden = hidden_grads.shape[1], hidden_grads.shape[2]
    dtype = activations.dtype
    flops = 2 * features * hidden * all_tokens
    total, acts, grads = pl.pallas_call(
        gather_kernel,
        out_shape=(
            pltpu.VMEM((features, hidden), jnp.float32),
            pltpu.VMEM((DEPTH, ROWS, tokens, features), dtype),
            pltpu.VMEM((DEPTH, all_tokens, hidden), dtype),
        ),
        in_specs=[pl.BlockSpec(memory_space=pl.ANY)] * 2,
        out_specs=(pl.BlockSpec(memory_space=pltpu.VMEM),) * 3,
        scratch_shapes=[
            pltpu.SemaphoreType.DMA((2,)),
            pltpu.SemaphoreType.DMA((DEPTH, ROWS)),
            pltpu.SemaphoreType.DMA((DEPTH, ROWS)),
            pltpu.SemaphoreType.DMA((DEPTH, ROWS)),
            pltpu.SemaphoreType.DMA((DEPTH, ROWS)),
            pltpu.SemaphoreType.DMA((3,)),
            pltpu.SemaphoreType.DMA((3, PARTS)),
            pltpu.SemaphoreType.DMA((3, PARTS)),
        ],
        compiler_params=pltpu.CompilerParams(
            collective_id=0, has_side_effects=True, vmem_limit_bytes=12 * MIB
        ),
        cost_estimate=pl.CostEstimate(flops=3 * flops, bytes_accessed=10 * MIB, transcendentals=0),
        name="gather",
    )(activations, hidden_grads)
    return pl.pallas_call(
        last_kernel,
        out_shape=jax.ShapeDtypeStruct((features, hidden), dtype),
        in_specs=[pl.BlockSpec(memory_space=pltpu.VMEM)] * 3,
        out_specs=pl.BlockSpec(memory_space=pl.ANY),
        scratch_shapes=[pltpu.VMEM((2, TILE, hidden), dtype), pltpu.SemaphoreType.DMA((2,))],
        compiler_params=pltpu.CompilerParams(vmem_limit_bytes=12 * MIB),
        cost_estimate=pl.CostEstimate(flops=flops, bytes_accessed=8 * MIB, transcendentals=0),
        name="last",
    )(total, acts, grads)


def by_ops(activations, hidden_grads):
    swapped = lax.all_to_all(activations, "depth", split_axis=2, concat_axis=0, tiled=True)
    acts = lax.all_gather(swapped, "row", axis=1, tiled=True)
    grads = lax.all_gather(hidden_grads, "depth", axis=0, tiled=True)
    grads = lax.all_gather(grads, "col", axis=1, tiled=True)
    total = lax.dot_general(
        acts, grads, (((0, 1), (0, 1)), ((), ())), preferred_element_type=jnp.float32
    )
    return total.astype(jnp.bfloat16)


def solution(mesh):
    in_specs = (P(("parts", "depth"), "row", "col"), P(("parts", "depth"), "col", "row"))
    out_specs = P(("parts", "col", "depth"), "row")
    sizes = (mesh.shape["row"], mesh.shape["col"], mesh.shape["depth"])
    local = by_kernels if sizes == (ROWS, COLS, DEPTH) else by_ops
    return jax.shard_map(local, mesh=mesh, in_specs=in_specs, out_specs=out_specs, check_vma=False)
```

time: 218 us -> 61.8 us (0.28)
  waiting for transfers between devices: 100 us -> 0 us
  Pallas kernels: 0 us -> 59.3 us
  other arithmetic: 45.2 us -> 0 us
  local copies, waits for them, and re-layouts: 31.2 us -> 2.27 us
  matrix products: 13.9 us -> 0 us
  between operations: 13.4 us -> 0.01 us
  blocking collectives: 12.9 us -> 0 us
    all_gather x2 -> x0, waiting for transfers between devices: 99.9 us -> none  [the longest x1 73.1 us: local(): acts = lax.all_gather(swapped, 'row', axis=1, tiled=True)]
    pallas_call x0 -> x2, Pallas kernels: none -> 59.3 us  [the longest x1 53.8 us: by_kernels(): pl.pallas_call(gather_kernel, out_shape=(pltpu.VMEM((features, hidden), j...]
    unnamed x1 -> x0, other arithmetic: 45.2 us -> none
    dot_general x1 -> x0, matrix products: 13.9 us -> none  [local(): lax.dot_general(acts, grads, (((0, 1), (0, 1)), ((), ())), preferred_elem...]
    all_to_all x1 -> x0, blocking collectives: 12.9 us -> none  [local(): lax.all_to_all(activations, 'depth', split_axis=2, concat_axis=0, tiled=T...]
    unnamed x4, local copies, waits for them, and re-layouts: 14.5 us -> 2.27 us
    all_to_all x2 -> x0, local copies, waits for them, and re-layouts: 9.14 us -> none  [local(): lax.all_to_all(activations, 'depth', split_axis=2, concat_axis=0, tiled=T...]
    all_gather x1 -> x0, local copies, waits for them, and re-layouts: 7.56 us -> none  [local(): acts = lax.all_gather(swapped, 'row', axis=1, tiled=True)]
  transfers between devices with their start and end apart: 2 -> 0, of which waited for: 2 -> 0; matrix products, arithmetic and copies ran while one was open for 3% -> 0% of each run, Pallas kernels for 0% -> 0%
where the time goes in v1:
time: 61.8 us; the launch traced here: 61.6 us
  Pallas kernels  59.3 us (96%)
  local copies, waits for them, and re-layouts  2.27 us (4%)
    pallas_call x1, Pallas kernels, by_kernels(): pl.pallas_call(gather_kernel, out_shape=(pltpu.VMEM((features, hidden), j...  53.8 us
    pallas_call x1, Pallas kernels, by_kernels(): pl.pallas_call(last_kernel, out_shape=jax.ShapeDtypeStruct((features, hid...  5.55 us
    unnamed x4, local copies, waits for them, and re-layouts  2.27 us

profile of v1, /device:TPU:0, one launch (start us, length us, event | category | flops | bytes accessed | tf_op | source)
XLA Modules:
  0.0 61.6 jit_solution(13764849131439865446)
XLA Ops:
  0.0 0.0 copy-start
  0.0 1.2 %copy-done = bf16[1,256,2048]{2,1,0:T(8,128)(2,1)S(1)} copy-done((bf16[1,256,2048]{2,1,0:T(8,128)(2,1)S(1)}, bf16[1,256,2048]{2,1,0:T(8,128)(2,1)}, u32[]{:S(2)}) %copy-start) | copy-done | bytes 1048600
  1.2 0.0 copy-start.1
  1.2 1.0 %copy-done.1 = bf16[1,32,8192]{2,1,0:T(8,128)(2,1)S(1)} copy-done((bf16[1,32,8192]{2,1,0:T(8,128)(2,1)S(1)}, bf16[1,32,8192]{2,1,0:T(8,128)(2,1)}, u32[]{:S(2)}) %copy-start.1) | copy-done | bytes 524312
  2.3 53.8 %gather.1 = (f32[2048,2048]{1,0:T(8,128)S(1)}, bf16[4,8,32,2048]{3,2,1,0:T(8,128)(2,1)S(1)}, bf16[4,256,2048]{2,1,0:T(8,128)(2,1)S(1)}) custom-call(bf16[1,32,8192]{2,1,0:T(8,128)(2,1)S(1)} %copy-done.1, bf16[1,256,2048]{2,1,0:T(8,128)(2,1)S(1)} %copy-done), custom_call_target="tpu_custom_call" | custom-call | flops 6442450944 | bytes 10485760 | tf_op jit(solution)/shard_map/gather/pallas_call | solution.py:268
  56.1 5.6 %last.1 = bf16[2048,2048]{1,0:T(8,128)(2,1)} custom-call(f32[2048,2048]{1,0:T(8,128)S(1)} %get-tuple-element.8.total, bf16[4,8,32,2048]{3,2,1,0:T(8,128)(2,1)S(1)} %get-tuple-element.9.acts, bf16[4,256,2048]{2,1,0:T(8,128)(2,1)S(1)} %get-tuple-element.10.grads), custom_call_target="tpu_custom_call" | custom-call | flops 2147483648 | bytes 8388608 | tf_op jit(solution)/shard_map/last/pallas_call | solution.py:293
Async XLA Ops:
  0.0 1.2 %copy-start = (bf16[1,256,2048]{2,1,0:T(8,128)(2,1)S(1)}, bf16[1,256,2048]{2,1,0:T(8,128)(2,1)}, u32[]{:S(2)}) copy-start(bf16[1,256,2048]{2,1,0:T(8,128)(2,1)} %g_hbm.1) | copy-start | bytes 3145732
  1.2 1.0 %copy-start.1 = (bf16[1,32,8192]{2,1,0:T(8,128)(2,1)S(1)}, bf16[1,32,8192]{2,1,0:T(8,128)(2,1)}, u32[]{:S(2)}) copy-start(bf16[1,32,8192]{2,1,0:T(8,128)(2,1)} %x_hbm.1) | copy-start | bytes 1572868

commit v2 on v1

--- a/solution.py
+++ b/solution.py
@@ -11,17 +11,23 @@
 MIB = 1024 * 1024
 ROWS, COLS, DEPTH = 8, 1, 4
 NZ = 4
+LAST_TILE, LAST_COPIES = 512, 4
 TILE = 256
 SHIFTED = (1, 3)
 PARTS = 2
 
 
+def columns(tile):
+    return pl.ds(pl.multiple_of(tile * TILE, TILE), TILE)
+
+
 def product_tile(acts, grads, slot, tile):
-    cols = pl.ds(pl.multiple_of(tile * TILE, TILE), TILE)
-    lhs = acts[slot, :, :, cols]
-    lhs = lhs.reshape(lhs.shape[0] * lhs.shape[1], TILE)
+    rows, tokens, width = acts.shape[1:]
     return lax.dot_general(
-        lhs, grads[slot], (((0,), (0,)), ((), ())), preferred_element_type=jnp.float32
+        acts[slot].reshape(rows * tokens, width),
+        grads[slot, :, columns(tile)],
+        (((0,), (0,)), ((), ())),
+        preferred_element_type=jnp.float32,
     )
 
 
@@ -120,8 +126,10 @@
     def own(j):
         moves(j, z, True, True, j > 0)()
 
-    def reach(j, dist):
+    def from_below(j, dist):
         pl.when(z >= dist)(moves(j, z - dist, True, False, True))
+
+    def from_above(j, dist):
         pl.when(z + dist < NZ)(moves(j, z + dist, False, True, True))
 
     def turn(j):
@@ -136,7 +144,7 @@
         def _():
             send(j, across, down_sem, here - 2).start()
 
-    def finish(j):
+    def ready(j):
         for origin in range(NZ):
             r = 2 * origin + 1 - y
             if j in SHIFTED:
@@ -145,62 +153,75 @@
                     arrived(j, r)
             else:
                 arrived(j, r)
+        if j == 0:
+            own_g.wait()
+        for p in range(PARTS):
+            if j == 1:
+                grads_to(1, p).wait_recv()
+            elif j == 3:
+                grads_on(p).wait_recv()
 
     def product(j, first, last):
         @pl.loop(first, last)
         def _(tile):
-            rows = pl.ds(pl.multiple_of(tile * TILE, TILE), TILE)
             value = product_tile(acts, grads, j, tile)
             if j == 0:
-                total[rows, :] = value
+                total[:, columns(tile)] = value
             else:
-                total[rows, :] = total[rows, :] + value
-
-    tiles = width // TILE
+                total[:, columns(tile)] = total[:, columns(tile)] + value
+
+    tiles = total.shape[1] // TILE
 
     own_x.wait()
     own(0)
-    exchange(1).start()
-    exchange(2).start()
-    exchange(3).start()
+    for k in (1, 2, 3):
+        exchange(k).start()
     for p in range(PARTS):
         grads_to(2, p).start()
     for p in range(PARTS):
         grads_to(1, p).start()
     own(1)
-    own_g.wait()
-    reach(0, 1)
+    from_above(0, 1)
     own(2)
-    reach(1, 1)
+    from_below(0, 1)
+    from_below(2, 1)
+    from_above(0, 2)
+    from_below(0, 2)
+    from_below(0, 3)
+    from_above(2, 1)
+    own(3)
+    from_below(2, 2)
+    from_above(0, 3)
+    from_below(1, 1)
+    from_above(2, 2)
+    from_below(2, 3)
+    from_above(1, 1)
+    from_above(2, 3)
+    from_above(1, 2)
+    from_below(1, 2)
+    ready(0)
+    product(0, 0 * tiles // 8, 1 * tiles // 8)
     turn(1)
-    reach(0, 2)
-    own(3)
-    reach(2, 1)
-    reach(1, 2)
-    reach(0, 3)
+    from_below(3, 1)
+    product(0, 1 * tiles // 8, 2 * tiles // 8)
+    from_above(3, 1)
+    product(0, 2 * tiles // 8, 8 * tiles // 8)
+    from_below(1, 3)
+    from_above(1, 3)
     forward_g(0)
+    forward_g(1)
+    ready(2)
+    product(2, 0 * tiles // 8, 4 * tiles // 8)
+    from_below(3, 2)
+    from_above(3, 2)
+    product(2, 4 * tiles // 8, 6 * tiles // 8)
     turn(3)
-    reach(3, 1)
-    finish(0)
-    product(0, 0, tiles // 4)
-    reach(2, 2)
-    product(0, tiles // 4, tiles // 2)
-    reach(1, 3)
-    product(0, tiles // 2, tiles)
-    forward_g(1)
-    reach(3, 2)
-    for p in range(PARTS):
-        grads_to(1, p).wait_recv()
-    finish(1)
-    product(1, 0, tiles // 2)
-    reach(2, 3)
-    product(1, tiles // 2, tiles)
-    reach(3, 3)
-    finish(2)
-    product(2, 0, tiles)
-    finish(3)
-    for p in range(PARTS):
-        grads_on(p).wait_recv()
+    product(2, 6 * tiles // 8, 8 * tiles // 8)
+    from_below(3, 3)
+    from_above(3, 3)
+    ready(1)
+    product(1, 0 * tiles // 8, 8 * tiles // 8)
+    ready(DEPTH - 1)
 
     for k in (1, 2, 3):
         exchange(k).wait_send()
@@ -237,27 +258,33 @@
 
 
 def last_kernel(total, acts, grads, out_hbm, held, sems):
-    tiles = total.shape[0] // TILE
-
-    def copy(tile, slot):
-        rows = pl.ds(pl.multiple_of(tile * TILE, TILE), TILE)
-        return pltpu.make_async_copy(held.at[slot], out_hbm.at[rows], sems.at[slot])
+    last = DEPTH - 1
+    rows, tokens = acts.shape[1:3]
+    tiles = total.shape[0] // LAST_TILE
+    part = LAST_TILE // LAST_COPIES
+
+    def copies(tile):
+        for p in range(LAST_COPIES):
+            some = pl.ds(pl.multiple_of(tile * LAST_TILE + p * part, part), part)
+            yield pltpu.make_async_copy(held.at[some], out_hbm.at[some], sems.at[tile, p])
 
     @pl.loop(0, tiles)
     def _(tile):
-        slot = tile % 2
-        rows = pl.ds(pl.multiple_of(tile * TILE, TILE), TILE)
-        value = total[rows, :] + product_tile(acts, grads, DEPTH - 1, tile)
-
-        @pl.when(tile >= 2)
-        def _():
-            copy(tile - 2, slot).wait()
-
-        held[slot] = value.astype(held.dtype)
-        copy(tile, slot).start()
-
-    for tile in (tiles - 2, tiles - 1):
-        copy(tile, tile % 2).wait()
+        some = pl.ds(pl.multiple_of(tile * LAST_TILE, LAST_TILE), LAST_TILE)
+        value = total[some, :] + lax.dot_general(
+            acts[last, :, :, some].reshape(rows * tokens, LAST_TILE),
+            grads[last],
+            (((0,), (0,)), ((), ())),
+            preferred_element_type=jnp.float32,
+        )
+        held[some, :] = value.astype(held.dtype)
+        for copy in copies(tile):
+            copy.start()
+
+    @pl.loop(0, tiles)
+    def _(tile):
+        for copy in copies(tile):
+            copy.wait()
 
 
 def by_kernels(activations, hidden_grads):
@@ -289,14 +316,20 @@
         ),
         cost_estimate=pl.CostEstimate(flops=3 * flops, bytes_accessed=10 * MIB, transcendentals=0),
         name="gather",
-    )(activations, hidden_grads)
+    )(
+        pltpu.with_memory_space_constraint(activations, pltpu.HBM),
+        pltpu.with_memory_space_constraint(hidden_grads, pltpu.HBM),
+    )
     return pl.pallas_call(
         last_kernel,
         out_shape=jax.ShapeDtypeStruct((features, hidden), dtype),
         in_specs=[pl.BlockSpec(memory_space=pltpu.VMEM)] * 3,
         out_specs=pl.BlockSpec(memory_space=pl.ANY),
-        scratch_shapes=[pltpu.VMEM((2, TILE, hidden), dtype), pltpu.SemaphoreType.DMA((2,))],
-        compiler_params=pltpu.CompilerParams(vmem_limit_bytes=12 * MIB),
+        scratch_shapes=[
+            pltpu.VMEM((features, hidden), dtype),
+            pltpu.SemaphoreType.DMA((features // LAST_TILE, LAST_COPIES)),
+        ],
+        compiler_params=pltpu.CompilerParams(vmem_limit_bytes=20 * MIB),
         cost_estimate=pl.CostEstimate(flops=flops, bytes_accessed=8 * MIB, transcendentals=0),
         name="last",
     )(total, acts, grads)

time: 61.8 us -> 53.6 us (0.87)
  Pallas kernels: 59.3 us -> 53.4 us
  local copies, waits for them, and re-layouts: 2.27 us -> 0 us
    pallas_call x1, Pallas kernels: 53.8 us -> 49 us  [by_kernels(): pl.pallas_call(gather_kernel, out_shape=(pltpu.VMEM((features, hidden), j...]
    unnamed x4 -> x0, local copies, waits for them, and re-layouts: 2.27 us -> none
    pallas_call x1, Pallas kernels: 5.55 us -> 4.43 us  [by_kernels(): pl.pallas_call(last_kernel, out_shape=jax.ShapeDtypeStruct((features, hid...]
where the time goes in v2:
time: 53.6 us; the launch traced here: 53.4 us
  Pallas kernels  53.4 us (100%)
    pallas_call x1, Pallas kernels, by_kernels(): pl.pallas_call(gather_kernel, out_shape=(pltpu.VMEM((features, hidden), j...  49 us
    pallas_call x1, Pallas kernels, by_kernels(): pl.pallas_call(last_kernel, out_shape=jax.ShapeDtypeStruct((features, hid...  4.43 us

profile of v2, /device:TPU:0, one launch (start us, length us, event | category | flops | bytes accessed | tf_op | source)
XLA Modules:
  0.0 53.4 jit_solution(5203926362795755184)
XLA Ops:
  0.0 49.0 %gather.1 = (f32[2048,2048]{1,0:T(8,128)S(1)}, bf16[4,8,32,2048]{3,2,1,0:T(8,128)(2,1)S(1)}, bf16[4,256,2048]{2,1,0:T(8,128)(2,1)S(1)}) custom-call(bf16[1,32,8192]{2,1,0:T(8,128)(2,1)} %x_hbm.1, bf16[1,256,2048]{2,1,0:T(8,128)(2,1)} %g_hbm.1), custom_call_target="tpu_custom_call" | custom-call | flops 6442450944 | bytes 10485760 | tf_op jit(solution)/shard_map/gather/pallas_call | solution.py:295
  49.0 4.4 %last.1 = bf16[2048,2048]{1,0:T(8,128)(2,1)} custom-call(f32[2048,2048]{1,0:T(8,128)S(1)} %get-tuple-element.8.total, bf16[4,8,32,2048]{3,2,1,0:T(8,128)(2,1)S(1)} %get-tuple-element.9.acts, bf16[4,256,2048]{2,1,0:T(8,128)(2,1)S(1)} %get-tuple-element.10.grads), custom_call_target="tpu_custom_call" | custom-call | flops 2147483648 | bytes 8388608 | tf_op jit(solution)/shard_map/last/pallas_call | solution.py:323
